TPU v7x, 32 devices: a whole 2x2x4 slice. The times are simulated.
32 devices in a mesh: grp: 2 (over x), ex: 16 (over z, y, core).
Axes of the slice: x: 2, y: 2, z: 4, core: 2. Of those that a mesh axis runs over, the one named last changes fastest.
Arguments:
- train_grads: bfloat16 [12288, 16384], P(('grp', 'ex')), parts along dimension 0, may hold values from -100 to 100
- queries: bfloat16 [2, 1024, 16384], P(None, ('grp', 'ex')), parts along dimension 1, may hold values from -6 to 6
- left_factor: bfloat16 [4, 64, 64], replicated, may hold values from -0.5 to 1.5
- right_factor: bfloat16 [4, 64, 64], replicated, may hold values from -0.5 to 1.5
Outputs:
- scores: float32 [12288, 1024], P(('grp', 'ex')), parts along dimension 0
There are 2 independent parts, one for each index of `grp`. A program takes and returns all parts, laid end to end along the dimension named above; an argument that names none is the same for every part. Nothing has to cross between parts.
All inputs are finite; a program needn't handle non-finite values.
Results may differ from a plain program's by a relative error of at most 0.0043.
Values may be sent and summed in bfloat16 or wider, within the bound.
A program may use at most 192 MiB of HBM per device.

v0:
```python
import functools

import jax
import jax.numpy as jnp
from jax import lax
from jax.experimental import pallas as pl
from jax.experimental.pallas import tpu as pltpu
from jax.sharding import PartitionSpec as P

PARTS = 4


def condition(gradients, left_factor, right_factor):
    modules, inner, _ = left_factor.shape
    outer = right_factor.shape[1]
    leading = gradients.shape[:-1]
    blocks_view = gradients.reshape(leading + (modules, inner, outer))
    halfway = jnp.einsum(
        "mij,...mjk->...mik", left_factor, blocks_view, preferred_element_type=jnp.float32
    )
    halfway = halfway.astype(jnp.bfloat16)
    full = jnp.einsum(
        "...mik,mkl->...mil", halfway, right_factor, preferred_element_type=jnp.float32
    )
    return full.reshape(leading + (modules * inner * outer,)).astype(jnp.bfloat16)


def ring_kernel(
    size, prepared_ref, train_ref, scores_ref, squares_ref,
    held, train, acc, flipped, mine, sums,
    own_sem, train_sem, send_sem, recv_sem, twin_send, twin_recv, sum_send, sum_recv,
):
    chips = size // 2
    rows = prepared_ref.shape[1]
    width = prepared_ref.shape[2] // PARTS
    block = size * rows
    me = lax.axis_index("ex")
    place, core = me // 2, lax.rem(me, 2)
    twin = place * 2 + 1 - core
    snake = size == 16

    def place_of(at):
        if not snake:
            return at
        side = at // (chips // 2)
        return 2 * (at + side * (chips - 1 - 2 * at)) + side

    at = place
    if snake:
        side, high = lax.rem(place, 2), place // 2
        at = high + side * (chips - 1 - 2 * high)
    ahead = place_of(lax.rem(at + 1, chips)) * 2 + core
    behind = place_of(lax.rem(at + chips - 1, chips)) * 2 + core

    def part(index):
        return pl.ds(index * width, width)

    def own_copy(way, index):
        return pltpu.make_async_copy(
            prepared_ref.at[way, :, part(index)],
            held.at[way, pl.ds(pl.multiple_of(me * rows, rows), rows), part(index)],
            own_sem.at[way, index],
        )

    def train_copy(index):
        return pltpu.make_async_copy(
            train_ref.at[:, part(index)], train.at[:, part(index)], train_sem.at[index]
        )

    for index in range(PARTS):
        for way in range(2):
            own_copy(way, index).start()
    for index in range(PARTS):
        train_copy(index).start()

    barrier = pltpu.get_barrier_semaphore()

    @pl.loop(1, size)
    def _(shift):
        pl.semaphore_signal(
            barrier, inc=1, device_id={"ex": lax.rem(me + shift, size)},
            device_id_type=pl.DeviceIdType.MESH,
        )

    pl.semaphore_wait(barrier, size - 1)

    def source(way, step):
        return place_of(lax.rem(at + (chips - step if way == 0 else step), chips))

    def slot(way, step, whose, index):
        start = (source(way, step) * 2 + whose) * rows
        return held.at[way, pl.ds(pl.multiple_of(start, rows), rows), part(index)]

    def forward(way, step, index):
        view = slot(way, step, core, index)
        return pltpu.make_async_remote_copy(
            src_ref=view, dst_ref=view,
            send_sem=send_sem.at[way, index], recv_sem=recv_sem.at[way, step, index],
            device_id={"ex": ahead if way == 0 else behind},
            device_id_type=pl.DeviceIdType.MESH,
        )

    def share(way, step, index):
        view = slot(way, step, core, index)
        return pltpu.make_async_remote_copy(
            src_ref=view, dst_ref=view,
            send_sem=twin_send.at[way, index], recv_sem=twin_recv.at[way, step, index],
            device_id={"ex": twin}, device_id_type=pl.DeviceIdType.MESH,
        )

    def arrived(way, step, whose, index, sem):
        view = slot(way, step, whose, index)
        pltpu.make_async_copy(view, view, sem).wait()

    @pl.loop(0, chips)
    def _(step):
        for index in range(PARTS):
            for way in range(2):
                @pl.when(step == 0)
                def _():
                    own_copy(way, index).wait()

                @pl.when(step > 0)
                def _():
                    arrived(way, step, core, index, recv_sem.at[way, step - 1, index])
                    forward(way, step - 1, index).wait_send()

                @pl.when(step < chips - 1)
                def _():
                    forward(way, step, index).start()

                @pl.when(step > 0)
                def _():
                    share(way, step - 1, index).wait_send()

                share(way, step, index).start()

            @pl.when(step == 0)
            def _():
                train_copy(index).wait()

            for way in range(2):
                arrived(way, step, 1 - core, index, twin_recv.at[way, step, index])
            pair = [
                held[way, pl.ds(pl.multiple_of(source(way, step) * 2 * rows, 2 * rows), 2 * rows), part(index)]
                for way in range(2)
            ]
            product = lax.dot_general(
                train[:, part(index)], jnp.concatenate(pair, axis=0),
                (((1,), (1,)), ((), ())), preferred_element_type=jnp.float32,
            )
            if index == 0:
                acc[...] = product
            elif index < PARTS - 1:
                acc[...] += product
            else:
                turned = (acc[...] + product).T
                for way in range(2):
                    start = way * block + source(way, step) * 2 * rows
                    flipped[pl.ds(pl.multiple_of(start, 2 * rows), 2 * rows), :] = turned[
                        way * 2 * rows : (way + 1) * 2 * rows
                    ]

    for index in range(PARTS):
        for way in range(2):
            share(way, chips - 1, index).wait_send()

    for start in range(0, 2 * block, 128):
        columns = flipped[start : start + 128, :].T
        scores_ref[:, start : start + 128] = columns
        mine[:, start : start + 128] = jnp.sum(columns * columns, axis=0, keepdims=True)

    def tell(shift):
        return pltpu.make_async_remote_copy(
            src_ref=mine, dst_ref=sums.at[shift],
            send_sem=sum_send.at[shift], recv_sem=sum_recv.at[shift],
            device_id={"ex": lax.rem(me + shift, size)},
            device_id_type=pl.DeviceIdType.MESH,
        )

    @pl.loop(1, size)
    def _(shift):
        tell(shift).start()

    sums[0] = mine[...]

    @pl.loop(1, size)
    def _(shift):
        tell(shift).wait()

    squares_ref[...] = jnp.sum(sums[...], axis=0)


def on_device(train_grads, queries, left_factor, right_factor):
    size = lax.axis_size("ex")
    count, features = train_grads.shape
    train_count = count * size
    prepared = condition(queries, left_factor, right_factor)
    blocks, rows, _ = queries.shape
    columns = blocks * size * rows
    chips = size // 2
    raw_scores, squares = pl.pallas_call(
        functools.partial(ring_kernel, size),
        out_shape=(
            jax.ShapeDtypeStruct((count, columns), jnp.float32),
            jax.ShapeDtypeStruct((1, columns), jnp.float32),
        ),
        in_specs=[pl.BlockSpec(memory_space=pl.ANY)] * 2,
        out_specs=(pl.BlockSpec(memory_space=pltpu.VMEM),) * 2,
        scratch_shapes=[
            pltpu.VMEM((2, size * rows, features), jnp.bfloat16),
            pltpu.VMEM((count, features), jnp.bfloat16),
            pltpu.VMEM((count, 4 * rows), jnp.float32),
            pltpu.VMEM((columns, count), jnp.float32),
            pltpu.VMEM((1, columns), jnp.float32),
            pltpu.VMEM((size, 1, columns), jnp.float32),
            pltpu.SemaphoreType.DMA((2, PARTS)),
            pltpu.SemaphoreType.DMA((PARTS,)),
            pltpu.SemaphoreType.DMA((2, PARTS)),
            pltpu.SemaphoreType.DMA((2, chips - 1, PARTS)),
            pltpu.SemaphoreType.DMA((2, PARTS)),
            pltpu.SemaphoreType.DMA((2, chips, PARTS)),
            pltpu.SemaphoreType.DMA((size,)),
            pltpu.SemaphoreType.DMA((size,)),
        ],
        compiler_params=pltpu.CompilerParams(
            collective_id=0, has_side_effects=True, vmem_limit_bytes=58 * 1024 * 1024
        ),
        cost_estimate=pl.CostEstimate(
            flops=2 * count * columns * features,
            bytes_accessed=2 * count * features + 4 * count * columns,
            transcendentals=0,
        ),
    )(prepared, train_grads)
    inverse_rms = lax.rsqrt(squares / train_count + 1e-06)
    return raw_scores * inverse_rms


def solution(mesh):
    in_specs = (P(("grp", "ex"), None), P(None, ("grp", "ex"), None), P(), P())
    out_specs = P(("grp", "ex"), None)
    return jax.shard_map(
        on_device, mesh=mesh, in_specs=in_specs, out_specs=out_specs, check_vma=False
    )
```

profile of v0, /device:TPU:0, one launch (start us, length us, event | category | flops | bytes accessed | tf_op | source)
XLA Modules:
  0.0 203.2 jit_solution(16631391689866004214)
XLA Ops:
  0.0 0.0 copy-start
  0.0 0.0 copy-start.1
  0.0 6.5 %reshape.5 = bf16[2,32,4,64,64]{4,3,2,1,0:T(8,128)(2,1)} reshape(bf16[2,32,16384]{2,1,0:T(8,128)(2,1)} %param.5) | data formatting | bytes 4194304 | tf_op jit(solution)/shard_map/reshape | solution.py:17
  6.5 0.0 copy-done
  6.5 0.0 copy-done.1
  6.5 6.5 %convert_bitcast_fusion = bf16[2,32,4,64,64]{4,3,1,0,2:T(8,128)(2,1)} fusion(bf16[2,32,4,64,64]{4,3,2,1,0:T(8,128)(2,1)} %reshape.5, bf16[4,64,64]{2,1,0:T(8,128)(2,1)S(1)} %copy-done, bf16[4,64,64]{2,1,0:T(8,128)(2,1)S(1)} %copy-done.1), kind=kOutput, calls=%fused_computation.4 | convolution fusion | flops 270532608 | bytes 4259840 | tf_op jit(solution)/shard_map/...mik,mkl->...mil/dot_general | solution.py:22
  13.0 5.6 %copy.5 = bf16[2,32,4,64,64]{4,3,2,1,0:T(8,128)(2,1)} copy(bf16[2,32,4,64,64]{4,3,1,0,2:T(8,128)(2,1)} %convert_bitcast_fusion) | data formatting | bytes 4194304 | tf_op jit(solution)/shard_map/convert_element_type | solution.py:25
  18.6 6.0 %convert_element_type.17.prepared_ref = bf16[2,32,16384]{2,1,0:T(8,128)(2,1)} reshape(bf16[2,32,4,64,64]{4,3,2,1,0:T(8,128)(2,1)} %copy.5) | data formatting | bytes 4194304 | tf_op jit(solution)/shard_map/convert_element_type | solution.py:25
  24.5 175.1 %shard_map.46 = (f32[384,1024]{1,0:T(8,128)}, f32[1,1024]{1,0:T(1,128)}) custom-call(bf16[2,32,16384]{2,1,0:T(8,128)(2,1)} %convert_element_type.17.prepared_ref, bf16[384,16384]{1,0:T(8,128)(2,1)} %train_ref.1), custom_call_target="tpu_custom_call" | custom-call | flops 12884901888 | bytes 14155776 | tf_op jit(solution)/shard_map/pallas_call | solution.py:202
  199.7 0.7 add_rsqrt_fusion
  200.4 2.8 %broadcast_multiply_fusion = f32[384,1024]{1,0:T(8,128)} fusion(f32[384,1024]{1,0:T(8,128)} %get-tuple-element.7, f32[1024]{0:T(1024)S(1)} %bitcast.21), kind=kLoop, calls=%fused_computation.6 | loop fusion | flops 393216 | bytes 3149824 | tf_op jit(solution)/shard_map/mul | solution.py:236
Async XLA Ops:
  0.0 6.5 %copy-start = (bf16[4,64,64]{2,1,0:T(8,128)(2,1)S(1)}, bf16[4,64,64]{2,1,0:T(8,128)(2,1)}, u32[]{:S(2)}) copy-start(bf16[4,64,64]{2,1,0:T(8,128)(2,1)} %param.7) | copy-start | bytes 98308
  0.0 6.5 %copy-start.1 = (bf16[4,64,64]{2,1,0:T(8,128)(2,1)S(1)}, bf16[4,64,64]{2,1,0:T(8,128)(2,1)}, u32[]{:S(2)}) copy-start(bf16[4,64,64]{2,1,0:T(8,128)(2,1)} %param.6) | copy-start | bytes 98308
where the time goes:
time: 204 us; the launch traced here: 203 us
  Pallas kernels  175 us (86%)
  local copies, waits for them, and re-layouts  18.1 us (9%)
  matrix products  6.47 us (3%)
  other arithmetic  3.5 us (2%)
    pallas_call x1, Pallas kernels, on_device(): pl.pallas_call(functools.partial(ring_kernel, size), out_shape=(jax.Shape...  175 us
    convert_element_type x2, local copies, waits for them, and re-layouts, condition(): full.reshape(leading + (modules * inner * outer,)).astype(jnp.bfloat16)  11.5 us
    reshape x1, local copies, waits for them, and re-layouts, condition(): blocks_view = gradients.reshape(leading + (modules, inner, outer))  6.51 us
    dot_general x1, matrix products, condition(): jnp.einsum('...mik,mkl->...mil', halfway, right_factor, preferred_element...  6.47 us

commit v1 on v0

v1 whole, which is shorter than its diff:
```python
import functools

import jax
import jax.numpy as jnp
from jax import lax
from jax.experimental import pallas as pl
from jax.experimental.pallas import tpu as pltpu
from jax.sharding import PartitionSpec as P

LANES = 128


def spread_left(left):
    inner = left.shape[0]
    half = inner // 2
    at = lax.broadcasted_iota(jnp.int32, (inner, inner), 0)
    of = lax.broadcasted_iota(jnp.int32, (inner, inner), 1)
    move = (of == jnp.where(at < half, 2 * at, 2 * (at - half) + 1)).astype(jnp.float32).astype(jnp.bfloat16)
    back = (at == jnp.where(of < half, 2 * of, 2 * (of - half) + 1)).astype(jnp.float32).astype(jnp.bfloat16)
    rows_moved = jnp.dot(move, left, preferred_element_type=jnp.float32).astype(jnp.bfloat16)
    return jnp.dot(rows_moved, back, preferred_element_type=jnp.float32).astype(jnp.bfloat16)


def spread_right(right):
    outer = right.shape[0]
    full = 4 * outer
    tall = lax.broadcasted_iota(jnp.int32, (full, outer), 0) & (outer - 1)
    down = (tall == lax.broadcasted_iota(jnp.int32, (full, outer), 1)).astype(jnp.float32).astype(jnp.bfloat16)
    wide = lax.broadcasted_iota(jnp.int32, (outer, full), 1) & (outer - 1)
    across = (wide == lax.broadcasted_iota(jnp.int32, (outer, full), 0)).astype(jnp.float32).astype(jnp.bfloat16)
    copies = jnp.dot(down, right, preferred_element_type=jnp.float32).astype(jnp.bfloat16)
    copies = jnp.dot(copies, across, preferred_element_type=jnp.float32)
    at = lax.broadcasted_iota(jnp.int32, (full, full), 0)
    of = lax.broadcasted_iota(jnp.int32, (full, full), 1)
    odd = (at >= 2 * outer) == ((of & outer) != 0)
    query = ((at & outer) != 0) == (of >= 2 * outer)
    return jnp.where(odd & query, copies, 0.0).astype(jnp.bfloat16)


def ring_kernel(
    size, count_all, queries_ref, train_ref, left_ref, right_ref, scores_ref,
    held, train, acc, flipped, mine, sums, raw, before, after,
    raw_sem, train_sem, send_sem, recv_sem, twin_send, twin_recv, sum_send, sum_recv,
):
    modules, inner, _ = left_ref.shape
    outer = right_ref.shape[1]
    half = inner // 2
    chips = size // 2
    rows = queries_ref.shape[1]
    width = inner * outer
    total = 2 * rows
    block = size * rows
    me = lax.axis_index("ex")
    place, core = me // 2, lax.rem(me, 2)
    twin = place * 2 + 1 - core
    snake = size == 16

    def place_of(at):
        if not snake:
            return at
        side = at // (chips // 2)
        return 2 * (at + side * (chips - 1 - 2 * at)) + side

    at = place
    if snake:
        side, high = lax.rem(place, 2), place // 2
        at = high + side * (chips - 1 - 2 * high)
    ahead = place_of(lax.rem(at + 1, chips)) * 2 + core
    behind = place_of(lax.rem(at + chips - 1, chips)) * 2 + core

    def part(index):
        return pl.ds(index * width, width)

    def raw_copy(index):
        return pltpu.make_async_copy(
            queries_ref.at[:, :, part(index)], raw.at[:, :, part(index)], raw_sem.at[index]
        )

    def train_copy(index):
        return pltpu.make_async_copy(
            train_ref.at[:, part(index)], train.at[:, part(index)], train_sem.at[index]
        )

    for index in range(modules):
        raw_copy(index).start()
    for index in range(modules):
        train_copy(index).start()

    barrier = pltpu.get_barrier_semaphore()

    @pl.loop(1, size)
    def _(shift):
        pl.semaphore_signal(
            barrier, inc=1, device_id={"ex": lax.rem(me + shift, size)},
            device_id_type=pl.DeviceIdType.MESH,
        )

    def source(way, step):
        return place_of(lax.rem(at + (chips - step if way == 0 else step), chips))

    def slot(way, step, whose, index):
        start = (source(way, step) * 2 + whose) * rows
        return held.at[way, pl.ds(pl.multiple_of(start, rows), rows), part(index)]

    def forward(way, step, index):
        view = slot(way, step, core, index)
        return pltpu.make_async_remote_copy(
            src_ref=view, dst_ref=view,
            send_sem=send_sem.at[way, index], recv_sem=recv_sem.at[way, step, index],
            device_id={"ex": ahead if way == 0 else behind},
            device_id_type=pl.DeviceIdType.MESH,
        )

    def share(way, step, index):
        view = slot(way, step, core, index)
        return pltpu.make_async_remote_copy(
            src_ref=view, dst_ref=view,
            send_sem=twin_send.at[way, index], recv_sem=twin_recv.at[way, step, index],
            device_id={"ex": twin}, device_id_type=pl.DeviceIdType.MESH,
        )

    def arrived(way, step, whose, index, sem):
        view = slot(way, step, whose, index)
        pltpu.make_async_copy(view, view, sem).wait()

    def condition(index):
        left = spread_left(left_ref[index])
        right = spread_right(right_ref[index])
        own = pl.ds(pl.multiple_of(me * rows, rows), rows)
        for pair in range(half):
            columns = pl.ds(index * width + pair * LANES, LANES)
            for way in range(2):
                before[pair * total + way * rows : pair * total + (way + 1) * rows, :] = raw[
                    way, :, columns
                ].astype(jnp.float32)

        group = 8

        @pl.loop(0, total, step=group)
        def _(first):
            low = lax.broadcasted_iota(jnp.int32, (half, LANES), 1) < outer
            stacks = []
            for query in range(0, group, 2):
                here = before[pl.ds(first + query, half, stride=total), :]
                there = before[pl.ds(first + query + 1, half, stride=total), :]
                even = jnp.where(low, here, pltpu.roll(there, outer, 1))
                odd = jnp.where(low, pltpu.roll(here, outer, 1), there)
                stacks.append(jnp.concatenate([even, odd], axis=0))
            stack = jnp.concatenate(stacks, axis=1).astype(jnp.bfloat16)
            halfway = jnp.dot(left, stack, preferred_element_type=jnp.float32).astype(jnp.bfloat16)
            sides = [
                jnp.concatenate(
                    [
                        halfway[:half, query * LANES : (query + 1) * LANES],
                        halfway[half:, query * LANES : (query + 1) * LANES],
                    ],
                    axis=1,
                )
                for query in range(group // 2)
            ]
            full = jnp.dot(jnp.concatenate(sides, axis=0), right, preferred_element_type=jnp.float32)
            for query in range(group):
                at_row, at_lane = query // 2 * half, query % 2 * LANES
                after[pl.ds(first + query, half, stride=total), :] = full[
                    at_row : at_row + half, at_lane : at_lane + LANES
                ]

        for pair in range(half):
            columns = pl.ds(index * width + pair * LANES, LANES)
            for way in range(2):
                held[way, own, columns] = after[
                    pair * total + way * rows : pair * total + (way + 1) * rows, :
                ].astype(jnp.bfloat16)

    def multiply(step, index):
        for way in range(2):
            arrived(way, step, 1 - core, index, twin_recv.at[way, step, index])
        pair = [
            held[way, pl.ds(pl.multiple_of(source(way, step) * total, total), total), part(index)]
            for way in range(2)
        ]
        product = lax.dot_general(
            train[:, part(index)], jnp.concatenate(pair, axis=0),
            (((1,), (1,)), ((), ())), preferred_element_type=jnp.float32,
        )
        if index == 0:
            acc[...] = product
        elif index < modules - 1:
            acc[...] += product
        else:
            turned = (acc[...] + product).T
            for way in range(2):
                start = way * block + source(way, step) * total
                flipped[pl.ds(pl.multiple_of(start, total), total), :] = turned[
                    way * total : (way + 1) * total
                ]

    for index in range(modules):
        raw_copy(index).wait()
        condition(index)
        if index == 0:
            pl.semaphore_wait(barrier, size - 1)
        for way in range(2):
            forward(way, 0, index).start()
            share(way, 0, index).start()

    for index in range(modules):
        train_copy(index).wait()
        multiply(0, index)

    def take(step, index, last):
        for way in range(2):
            arrived(way, step, core, index, recv_sem.at[way, step - 1, index])
            forward(way, step - 1, index).wait_send()
            if not last:
                forward(way, step, index).start()
            share(way, step - 1, index).wait_send()
            share(way, step, index).start()

    @pl.loop(1, chips - 1)
    def _(step):
        for index in range(modules):
            take(step, index, False)
            multiply(step, index)

    def finish(start):
        columns = flipped[pl.ds(start, LANES), :].T
        scores_ref[:, pl.ds(start, LANES)] = columns
        mine[:, pl.ds(start, LANES)] = jnp.sum(columns * columns, axis=0, keepdims=True)

    late = [
        way * (block // LANES) + source(way, chips - 1) * total // LANES for way in range(2)
    ]
    for index in range(modules):
        take(chips - 1, index, True)
        multiply(chips - 1, index)
        if index == 0:
            @pl.loop(0, 2 * block // LANES)
            def _(chunk):
                @pl.when((chunk != late[0]) & (chunk != late[1]))
                def _():
                    finish(pl.multiple_of(chunk * LANES, LANES))

    for way in range(2):
        finish(pl.multiple_of(late[way] * LANES, LANES))

    def tell(shift):
        return pltpu.make_async_remote_copy(
            src_ref=mine, dst_ref=sums.at[shift],
            send_sem=sum_send.at[shift], recv_sem=sum_recv.at[shift],
            device_id={"ex": lax.rem(me + shift, size)},
            device_id_type=pl.DeviceIdType.MESH,
        )

    @pl.loop(1, size)
    def _(shift):
        tell(shift).start()

    sums[0] = mine[...]
    for index in range(modules):
        for way in range(2):
            share(way, chips - 1, index).wait_send()

    @pl.loop(1, size)
    def _(shift):
        tell(shift).wait()

    inverse_rms = lax.rsqrt(jnp.sum(sums[...], axis=0) / count_all + 1e-06)
    scores_ref[...] = scores_ref[...] * inverse_rms


def on_device(train_grads, queries, left_factor, right_factor):
    size = lax.axis_size("ex")
    count, features = train_grads.shape
    blocks, rows, _ = queries.shape
    modules, inner, _ = left_factor.shape
    columns = blocks * size * rows
    chips = size // 2
    strip = (inner // 2 * 2 * rows, LANES)
    return pl.pallas_call(
        functools.partial(ring_kernel, size, count * size),
        out_shape=jax.ShapeDtypeStruct((count, columns), jnp.float32),
        in_specs=[pl.BlockSpec(memory_space=pl.ANY)] * 2 + [pl.BlockSpec(memory_space=pltpu.VMEM)] * 2,
        out_specs=pl.BlockSpec(memory_space=pltpu.VMEM),
        scratch_shapes=[
            pltpu.VMEM((2, size * rows, features), jnp.bfloat16),
            pltpu.VMEM((count, features), jnp.bfloat16),
            pltpu.VMEM((count, 4 * rows), jnp.float32),
            pltpu.VMEM((columns, count), jnp.float32),
            pltpu.VMEM((1, columns), jnp.float32),
            pltpu.VMEM((size, 1, columns), jnp.float32),
            pltpu.VMEM((2, rows, features), jnp.bfloat16),
            pltpu.VMEM(strip, jnp.float32),
            pltpu.VMEM(strip, jnp.float32),
            pltpu.SemaphoreType.DMA((modules,)),
            pltpu.SemaphoreType.DMA((modules,)),
            pltpu.SemaphoreType.DMA((2, modules)),
            pltpu.SemaphoreType.DMA((2, chips - 1, modules)),
            pltpu.SemaphoreType.DMA((2, modules)),
            pltpu.SemaphoreType.DMA((2, chips, modules)),
            pltpu.SemaphoreType.DMA((size,)),
            pltpu.SemaphoreType.DMA((size,)),
        ],
        compiler_params=pltpu.CompilerParams(
            collective_id=0, has_side_effects=True, vmem_limit_bytes=60 * 1024 * 1024
        ),
        cost_estimate=pl.CostEstimate(
            flops=2 * count * columns * features,
            bytes_accessed=2 * count * features + 4 * count * columns,
            transcendentals=0,
        ),
    )(queries, train_grads, left_factor, right_factor)


def solution(mesh):
    in_specs = (P(("grp", "ex"), None), P(None, ("grp", "ex"), None), P(), P())
    out_specs = P(("grp", "ex"), None)
    return jax.shard_map(
        on_device, mesh=mesh, in_specs=in_specs, out_specs=out_specs, check_vma=False
    )
```

time: 204 us -> 182 us (0.89)
  local copies, waits for them, and re-layouts: 18.1 us -> 2.73 us
  matrix products: 6.47 us -> 0 us
  Pallas kernels: 175 us -> 179 us
  other arithmetic: 3.5 us -> 0 us
    convert_element_type x2 -> x0, local copies, waits for them, and re-layouts: 11.5 us -> none  [condition(): full.reshape(leading + (modules * inner * outer,)).astype(jnp.bfloat16)]
    reshape x1 -> x0, local copies, waits for them, and re-layouts: 6.51 us -> none  [condition(): blocks_view = gradients.reshape(leading + (modules, inner, outer))]
    dot_general x1 -> x0, matrix products: 6.47 us -> none  [condition(): jnp.einsum('...mik,mkl->...mil', halfway, right_factor, preferred_element...]
    pallas_call x1, Pallas kernels: 175 us -> 179 us  [on_device(): pl.pallas_call(functools.partial(ring_kernel, size, count * size), out_sh...]
    mul x1 -> x0, other arithmetic: 2.81 us -> none  [on_device(): return raw_scores * inverse_rms]
    unnamed x4 -> x1, local copies, waits for them, and re-layouts: 0.01 us -> 2.73 us
where the time goes in v1:
time: 182 us; the launch traced here: 181 us
  Pallas kernels  179 us (98%)
  local copies, waits for them, and re-layouts  2.73 us (2%)
    pallas_call x1, Pallas kernels, on_device(): pl.pallas_call(functools.partial(ring_kernel, size, count * size), out_sh...  179 us

profile of v1, /device:TPU:0, one launch (start us, length us, event | category | flops | bytes accessed | tf_op | source)
XLA Modules:
  0.0 181.5 jit_solution(13620657847435815806)
XLA Ops:
  0.0 178.7 %shard_map.46 = f32[384,1024]{1,0:T(8,128)} custom-call(bf16[2,32,16384]{2,1,0:T(8,128)(2,1)} %queries_ref.1, bf16[384,16384]{1,0:T(8,128)(2,1)} %train_ref.1, bf16[4,64,64]{2,1,0:T(8,128)(2,1)} %left_ref.1, bf16[4,64,64]{2,1,0:T(8,128)(2,1)} %right_ref.1), custom_call_target="tpu_custom_call" | custom-call | flops 12884901888 | bytes 14155776 | tf_op jit(solution)/shard_map/pallas_call | solution.py:280
  178.7 2.7 %copy.6 = f32[384,1024]{1,0:T(8,128)} copy(f32[384,1024]{1,0:T(8,128)} %shard_map.46) | data formatting | bytes 3145728

commit v2 on v1

--- a/solution.py
+++ b/solution.py
@@ -123,20 +123,17 @@
         view = slot(way, step, whose, index)
         pltpu.make_async_copy(view, view, sem).wait()
 
-    def condition(index):
-        left = spread_left(left_ref[index])
-        right = spread_right(right_ref[index])
+    def condition(index, way, left, right):
         own = pl.ds(pl.multiple_of(me * rows, rows), rows)
         for pair in range(half):
             columns = pl.ds(index * width + pair * LANES, LANES)
-            for way in range(2):
-                before[pair * total + way * rows : pair * total + (way + 1) * rows, :] = raw[
-                    way, :, columns
-                ].astype(jnp.float32)
+            before[pair * total + way * rows : pair * total + (way + 1) * rows, :] = raw[
+                way, :, columns
+            ].astype(jnp.float32)
 
         group = 8
 
-        @pl.loop(0, total, step=group)
+        @pl.loop(way * rows, (way + 1) * rows, step=group)
         def _(first):
             low = lax.broadcasted_iota(jnp.int32, (half, LANES), 1) < outer
             stacks = []
@@ -167,10 +164,9 @@
 
         for pair in range(half):
             columns = pl.ds(index * width + pair * LANES, LANES)
-            for way in range(2):
-                held[way, own, columns] = after[
-                    pair * total + way * rows : pair * total + (way + 1) * rows, :
-                ].astype(jnp.bfloat16)
+            held[way, own, columns] = after[
+                pair * total + way * rows : pair * total + (way + 1) * rows, :
+            ].astype(jnp.bfloat16)
 
     def multiply(step, index):
         for way in range(2):
@@ -197,10 +193,12 @@
 
     for index in range(modules):
         raw_copy(index).wait()
-        condition(index)
-        if index == 0:
-            pl.semaphore_wait(barrier, size - 1)
+        left = spread_left(left_ref[index])
+        right = spread_right(right_ref[index])
         for way in range(2):
+            condition(index, way, left, right)
+            if index == 0 and way == 0:
+                pl.semaphore_wait(barrier, size - 1)
             forward(way, 0, index).start()
             share(way, 0, index).start()
 

time: 182 us -> 181 us (level)
  no operation moved by 1% of the time
where the time goes in v2:
time: 181 us
  Pallas kernels  178 us (98%)
  local copies, waits for them, and re-layouts  2.73 us (2%)
    pallas_call x1, Pallas kernels, on_device(): pl.pallas_call(functools.partial(ring_kernel, size, count * size), out_sh...  178 us

profile of v2, /device:TPU:0, one launch (start us, length us, event | category | flops | bytes accessed | tf_op | source)
XLA Modules:
  0.0 180.8 jit_solution(15027488287482677710)
XLA Ops:
  0.0 178.1 %shard_map.46 = f32[384,1024]{1,0:T(8,128)} custom-call(bf16[2,32,16384]{2,1,0:T(8,128)(2,1)} %queries_ref.1, bf16[384,16384]{1,0:T(8,128)(2,1)} %train_ref.1, bf16[4,64,64]{2,1,0:T(8,128)(2,1)} %left_ref.1, bf16[4,64,64]{2,1,0:T(8,128)(2,1)} %right_ref.1), custom_call_target="tpu_custom_call" | custom-call | flops 12884901888 | bytes 14155776 | tf_op jit(solution)/shard_map/pallas_call | solution.py:278
  178.1 2.7 %copy.6 = f32[384,1024]{1,0:T(8,128)} copy(f32[384,1024]{1,0:T(8,128)} %shard_map.46) | data formatting | bytes 3145728
